TPU v7x, 32 devices: a whole 2x2x4 slice. The times are simulated.
32 devices in a mesh: mode: 8 (over z, core), cols: 4 (over y, x).
Axes of the slice: x: 2, y: 2, z: 4, core: 2. Of those that a mesh axis runs over, the one named last changes fastest.
Arguments:
- snapshots: float32 [512, 32768], P('mode', 'cols'), may hold values from -54 to 54, as said below
- start_basis: float32 [512, 128], replicated, may hold values from -6 to 6
Outputs:
- subspace_basis: float32 [512, 128], replicated
- core_tensor: float32 [128, 32768], P('mode', 'cols')
Inputs may be any that keep to these rules, and one draw needn't show every extreme that they name: `snapshots`: entries are finite real values.
All inputs are finite; a program needn't handle non-finite values.
Results may differ from a plain program's by a relative error of at most 0.00017.
Values sent between devices are 32-bit elements; how exact they have to be, the bound alone decides.
A program may use at most 64 MiB of HBM per device.

v0:
```python
import jax
import jax.numpy as jnp
from jax import lax
from jax.sharding import PartitionSpec as P


def orthonormal(projected):
    current = projected
    for sweep in range(2):
        inner = jnp.dot(
            current.T, current, precision=lax.Precision.HIGHEST, preferred_element_type=jnp.float32
        )
        lower_part = jnp.linalg.cholesky(inner)
        current = jax.scipy.linalg.solve_triangular(lower_part, current.T, lower=True).T
    return current


def shards(snapshots, start_basis):
    fibres = lax.all_to_all(snapshots, "mode", split_axis=1, concat_axis=0, tiled=True)
    local_gram = jnp.dot(
        fibres, fibres.T, precision=lax.Precision.HIGHEST, preferred_element_type=jnp.float32
    )
    gram_whole = lax.psum(local_gram, ("mode", "cols"))
    projected = jnp.dot(
        gram_whole, start_basis, precision=lax.Precision.HIGHEST, preferred_element_type=jnp.float32
    )
    subspace_basis = orthonormal(projected)
    core_local = jnp.dot(
        subspace_basis.T,
        fibres,
        precision=lax.Precision.HIGHEST,
        preferred_element_type=jnp.float32,
    )
    core_tensor = lax.all_to_all(core_local, "mode", split_axis=0, concat_axis=1, tiled=True)
    return (subspace_basis, core_tensor)


def solution(mesh):
    return jax.shard_map(
        shards,
        mesh=mesh,
        in_specs=(P("mode", "cols"), P()),
        out_specs=(P(), P("mode", "cols")),
        check_vma=False,
    )
```

profile of v0, /device:TPU:0, one launch (start us, length us, event | category | flops | bytes accessed | tf_op | source)
XLA Modules:
  0.0 276.5 jit_solution(1459549177347681278)
XLA Ops:
  7.2 1.8 copy.16
  9.0 55.2 %all_to_all.35 = f32[64,8,1024]{2,0,1:T(8,128)S(1)} all-to-all(f32[64,8,1024]{2,0,1:T(8,128)S(1)} %bitcast.48), channel_id=1, replica_groups=mesh['mode'=8,'cols'=4] {'mode'}, dimensions={1} | all-to-all | bytes 4194304 | tf_op jit(solution)/shard_map/all_to_all | solution.py:19
  64.2 4.6 %fusion.11 = f32[512,512]{1,0:T(8,128)} fusion(f32[512,1024]{1,0:T(8,128)S(1)} %bitcast.46), kind=kOutput, calls=%fused_computation.21 | convolution fusion | flops 3221225472 | bytes 3145728 | tf_op jit(solution)/shard_map/dot_general | solution.py:20
  68.8 128.9 %all-reduce.2.cloned.1.call-done = f32[512,512]{1,0:T(8,128)} async-done(((f32[512,512]{1,0:T(8,128)}), f32[512,512]{1,0:T(8,128)}) %all-reduce.2.cloned.1.call-update) | async-done | bytes 1048592 | tf_op jit(solution)/shard_map/psum | solution.py:23
  197.7 2.2 fusion.12
  199.9 0.6 fusion.13
  200.5 0.1 copy.9
  200.6 11.7 %cholesky.44 = f32[128,128]{1,0:T(8,128)S(1)} custom-call(f32[128,128]{1,0:T(8,128)S(1)} %fusion.8), custom_call_target="Cholesky" | custom-call | tf_op jit(solution)/shard_map/jit(cholesky)/cholesky | solution.py:13
  212.4 0.6 compare_reduce_fusion.1
  213.0 0.7 fusion.2
  213.7 9.8 %custom-call.6 = f32[1,128,128]{1,2,0:T(8,128)S(1)} custom-call(f32[1,128,128]{2,1,0:T(8,128)S(1)} %fusion.2), custom_call_target="InvertDiagBlocksLowerTriangular" | custom-call | tf_op jit(solution)/shard_map/jit(_solve_triangular)/triangular_solve | solution.py:14
  223.5 0.4 fusion
  223.9 0.6 fusion.14
  224.5 0.1 copy.10
  224.6 11.7 %cholesky.55 = f32[128,128]{1,0:T(8,128)S(1)} custom-call(f32[128,128]{1,0:T(8,128)S(1)} %fusion.6), custom_call_target="Cholesky" | custom-call | tf_op jit(solution)/shard_map/jit(cholesky)/cholesky | solution.py:13
  236.3 0.6 compare_reduce_fusion
  237.0 0.7 fusion.3
  237.6 9.8 %custom-call.7 = f32[1,128,128]{1,2,0:T(8,128)S(1)} custom-call(f32[1,128,128]{2,1,0:T(8,128)S(1)} %fusion.3), custom_call_target="InvertDiagBlocksLowerTriangular" | custom-call | tf_op jit(solution)/shard_map/jit(_solve_triangular)/triangular_solve | solution.py:14
  247.4 0.4 fusion.4
  247.9 2.1 fusion.15
  250.0 3.5 %all-to-all-start.1 = ((f32[8,16,1024]{2,1,0:T(8,128)}), f32[8,16,1024]{2,1,0:T(8,128)S(1)}, u32[]{:S(2)}, u32[]{:S(2)}) async-start(f32[8,16,1024]{2,1,0:T(8,128)} %fusion.15), calls=%async_computation.1 | async-start | bytes 1048576 | tf_op jit(solution)/shard_map/all_to_all | solution.py:34
  253.5 0.8 copy.12
  254.3 14.5 %all-to-all-done.1 = f32[8,16,1024]{2,1,0:T(8,128)S(1)} async-done(((f32[8,16,1024]{2,1,0:T(8,128)}), f32[8,16,1024]{2,1,0:T(8,128)S(1)}, u32[]{:S(2)}, u32[]{:S(2)}) %all-to-all-start.1) | async-done | bytes 524320 | tf_op jit(solution)/shard_map/all_to_all | solution.py:34
  268.8 0.8 copy.14
  (8 shorter events, 0.2 us)
Async XLA Ops:
  7.2 190.5 %copy-start = (f32[512,128]{1,0:T(8,128)S(1)}, f32[512,128]{1,0:T(8,128)}, u32[]{:S(2)}) copy-start(f32[512,128]{1,0:T(8,128)} %param.6) | copy-start | bytes 786436
  7.2 190.5 %all-reduce.2.cloned.1.call-start = ((), (), s32[]{:S(2)}) async-start(), calls=%async_computation.2 | async-start | bytes 2097152 | tf_op jit(solution)/shard_map/psum | solution.py:23
  250.0 18.9 %all-to-all-start.1 = ((f32[8,16,1024]{2,1,0:T(8,128)}), f32[8,16,1024]{2,1,0:T(8,128)S(1)}, u32[]{:S(2)}, u32[]{:S(2)}) async-start(f32[8,16,1024]{2,1,0:T(8,128)} %fusion.15), calls=%async_computation.1 | async-start | bytes 1048576 | tf_op jit(solution)/shard_map/all_to_all | solution.py:34
Sparse Core Ops, SparseCore 0:
  68.9 128.7 all-reduce.1
where the time goes:
time: 277 us
  waiting for transfers between devices  143 us (52%)
  blocking collectives  55.2 us (20%)
  other arithmetic  45.7 us (16%)
  between operations  14.1 us (5%)
  matrix products  10.8 us (4%)
  local copies, waits for them, and re-layouts  3.62 us (1%)
  starting transfers between devices  3.56 us (1%)
    psum x1, waiting for transfers between devices, shards(): gram_whole = lax.psum(local_gram, ('mode', 'cols'))  129 us
    all_to_all x1, blocking collectives, shards(): lax.all_to_all(snapshots, 'mode', split_axis=1, concat_axis=0, tiled=True)  55.2 us
    another operation x6, other arithmetic, orthonormal(): lower_part = jnp.linalg.cholesky(inner)  24.8 us
    another operation x4, other arithmetic, orthonormal(): jax.scipy.linalg.solve_triangular(lower_part, current.T, lower=True)  20.9 us
    all_to_all x1, waiting for transfers between devices, shards(): lax.all_to_all(core_local, 'mode', split_axis=0, concat_axis=1, tiled=True)  14.5 us
  transfers between devices with their start and end apart: 2, of which 2 were waited for; matrix products, arithmetic and copies ran while one was open for 0% of the time, Pallas kernels for 0%

commit v1 on v0

v1 whole, which is shorter than its diff:
```python
import functools

import jax
import jax.numpy as jnp
from jax import lax
from jax.experimental import pallas as pl
from jax.experimental.pallas import tpu as pltpu
from jax.sharding import PartitionSpec as P

MESH = pl.DeviceIdType.MESH
SUB = 8


def dot(a, b, dims):
    return lax.dot_general(
        a,
        b,
        (dims, ((), ())),
        precision=lax.Precision.HIGHEST,
        preferred_element_type=jnp.float32,
    )


def greet(modes, cols):
    me, mc = lax.axis_index("mode"), lax.axis_index("cols")
    barrier = pltpu.get_barrier_semaphore()
    for d in range(1, modes):
        pl.semaphore_signal(
            barrier, inc=1, device_id={"mode": lax.rem(me + d, modes)}, device_id_type=MESH
        )
    for d in range(1, cols):
        pl.semaphore_signal(
            barrier, inc=1, device_id={"cols": lax.rem(mc + d, cols)}, device_id_type=MESH
        )
    pl.semaphore_wait(barrier, modes - 1 + cols - 1)


def gather_kernel(
    modes, cols, parts,
    x_ref, b_ref, f_ref, p_ref,
    part, piece, slots_c, slots_m,
    own_sem, s0, r0, s1, r1, s2, r2, s3, r3, s4, r4,
):
    me, mc = lax.axis_index("mode"), lax.axis_index("cols")
    rows = x_ref.shape[0]
    width = f_ref.shape[1]
    cw = width // parts
    whole = f_ref.shape[0]

    def put(src, dst, send, recv, axis, peer):
        return pltpu.make_async_remote_copy(
            src_ref=src, dst_ref=dst, send_sem=send, recv_sem=recv,
            device_id={axis: peer}, device_id_type=MESH,
        )

    my_rows = pl.ds(pl.multiple_of(me * rows, rows), rows)
    own = []
    for k in range(parts):
        copy = pltpu.make_async_copy(
            x_ref.at[:, pl.ds(pl.multiple_of(me * width + k * cw, cw), cw)],
            f_ref.at[my_rows, pl.ds(k * cw, cw)],
            own_sem.at[k],
        )
        copy.start()
        own.append(copy)

    greet(modes, cols)

    sent = []
    for k in range(parts):
        row = []
        for d in range(modes - 1, 0, -1):
            peer = lax.rem(me + d, modes)
            copy = put(
                x_ref.at[:, pl.ds(pl.multiple_of(peer * width + k * cw, cw), cw)],
                f_ref.at[my_rows, pl.ds(k * cw, cw)],
                s0.at[k * (modes - 1) + d - 1], r0.at[k * (modes - 1) + d - 1], "mode", peer,
            )
            copy.start()
            row.append(copy)
        sent.append(row)

    bt = b_ref[...].T
    for k in range(parts):
        own[k].wait()
        for copy in sent[k]:
            copy.wait_recv()
        fk = f_ref[:, pl.ds(k * cw, cw)]
        t = dot(bt, fk, ((1,), (0,)))
        term = dot(fk, t, ((1,), (1,)))
        if k == 0:
            part[...] = term
        else:
            part[...] += term

    rc = whole // cols
    mine = pl.ds(pl.multiple_of(mc * rc, rc), rc)
    first = []
    for d in range(1, cols):
        peer = lax.rem(mc + d, cols)
        copy = put(
            part.at[pl.ds(pl.multiple_of(peer * rc, rc), rc)],
            slots_c.at[d - 1], s1.at[d - 1], r1.at[d - 1], "cols", peer,
        )
        copy.start()
        first.append(copy)
    for copy in first:
        copy.wait_recv()
    total = part[mine, :]
    for d in range(1, cols):
        total = total + slots_c[d - 1]
    piece[...] = total

    sl = slots_m.shape[1]
    owners = rc // sl

    def guarded(flag, body):
        if owners == modes:
            body()
        else:
            pl.when(flag)(body)

    second = []
    for d in range(1, modes):
        peer = lax.rem(me + d, modes)
        place = peer if owners == modes else lax.rem(peer, owners)
        copy = put(
            piece.at[pl.ds(pl.multiple_of(place * sl, sl), sl)],
            slots_m.at[d - 1], s2.at[d - 1], r2.at[d - 1], "mode", peer,
        )
        guarded(peer < owners, copy.start)
        second.append((copy, peer))
    for copy, _ in second:
        guarded(me < owners, copy.wait_recv)
    place = me if owners == modes else lax.rem(me, owners)
    target = pl.ds(pl.multiple_of(mc * rc + place * sl, sl), sl)

    def add():
        total = piece[pl.ds(pl.multiple_of(place * sl, sl), sl), :]
        for d in range(1, modes):
            total = total + slots_m[d - 1]
        p_ref[target, :] = total

    guarded(me < owners, add)

    third = []
    for d in range(1, modes):
        peer = lax.rem(me + d, modes)
        copy = put(p_ref.at[target], p_ref.at[target], s3.at[d - 1], r3.at[d - 1], "mode", peer)
        guarded(me < owners, copy.start)
        third.append(copy)
    for d in range(1, modes):
        source = lax.rem(me + modes - d, modes)
        guarded(source < owners, third[d - 1].wait_recv)
    fourth = []
    for d in range(1, cols):
        peer = lax.rem(mc + d, cols)
        copy = put(p_ref.at[mine], p_ref.at[mine], s4.at[d - 1], r4.at[d - 1], "cols", peer)
        copy.start()
        fourth.append(copy)
    for copy in fourth:
        copy.wait_recv()

    for row in sent:
        for copy in row:
            copy.wait_send()
    for copy in first:
        copy.wait_send()
    for copy, peer in second:
        guarded(peer < owners, copy.wait_send)
    for copy in third:
        guarded(me < owners, copy.wait_send)
    for copy in fourth:
        copy.wait_send()


def gather(modes, cols, x, b):
    rows, local = x.shape
    whole, width = rows * modes, local // modes
    rank = b.shape[1]
    parts = 2 if width % 256 == 0 else 1
    rc = whole // cols
    sl = max(SUB, rc // modes)
    dma = pltpu.SemaphoreType.DMA
    vmem = pl.BlockSpec(memory_space=pltpu.VMEM)
    return pl.pallas_call(
        functools.partial(gather_kernel, modes, cols, parts),
        out_shape=(
            jax.ShapeDtypeStruct((whole, width), jnp.float32),
            jax.ShapeDtypeStruct((whole, rank), jnp.float32),
        ),
        in_specs=[pl.BlockSpec(memory_space=pl.ANY), vmem],
        out_specs=(vmem, vmem),
        scratch_shapes=[
            pltpu.VMEM((whole, rank), jnp.float32),
            pltpu.VMEM((rc, rank), jnp.float32),
            pltpu.VMEM((cols - 1, rc, rank), jnp.float32),
            pltpu.VMEM((modes - 1, sl, rank), jnp.float32),
            dma((parts,)),
            dma((parts * (modes - 1),)), dma((parts * (modes - 1),)),
            dma((cols - 1,)), dma((cols - 1,)),
            dma((modes - 1,)), dma((modes - 1,)),
            dma((modes - 1,)), dma((modes - 1,)),
            dma((cols - 1,)), dma((cols - 1,)),
        ],
        compiler_params=pltpu.CompilerParams(
            collective_id=0, has_side_effects=True, vmem_limit_bytes=32 * 2**20
        ),
        name="gather_project",
    )(x, b)


def inverse_factor(a, out_ref):
    n = a.shape[0]
    count = n // SUB
    shape = (SUB, n)
    row_id = lax.broadcasted_iota(jnp.int32, shape, 0)
    col_id = lax.broadcasted_iota(jnp.int32, shape, 1)
    blocks = [a[SUB * i:SUB * (i + 1), :] for i in range(count)]
    duals = [
        jnp.where(col_id == row_id + SUB * i, 1.0, 0.0).astype(jnp.float32) for i in range(count)
    ]
    for j in range(0, n, 2):
        at, jj = j // SUB, j % SUB
        block, dual = blocks[at], duals[at]
        u0, u1 = (jnp.broadcast_to(block[jj + i:jj + i + 1, :], shape) for i in range(2))
        v0, v1 = (jnp.broadcast_to(dual[jj + i:jj + i + 1, :], shape) for i in range(2))
        p = jnp.broadcast_to(u0[:, j:j + 1], shape)
        q = jnp.broadcast_to(u0[:, j + 1:j + 2], shape)
        r = jnp.broadcast_to(u1[:, j + 1:j + 2], shape)
        idet = 1.0 / (p * r - q * q)
        i00, i01, i11 = r * idet, -q * idet, p * idet
        x0, x1 = i00 * u0 + i01 * u1, i01 * u0 + i11 * u1
        y0, y1 = i00 * v0 + i01 * v1, i01 * v0 + i11 * v1
        out_ref[j:j + 1, :] = (v0 * lax.rsqrt(p))[0:1, :]
        out_ref[j + 1:j + 2, :] = ((v1 - (q / p) * v0) * jnp.sqrt(i11))[0:1, :]
        for i in range(at, count):
            c0 = jnp.broadcast_to(blocks[i][:, j:j + 1], shape)
            c1 = jnp.broadcast_to(blocks[i][:, j + 1:j + 2], shape)
            if i == at:
                if jj + 2 == SUB:
                    continue
                later = row_id > jj + 1
                c0, c1 = jnp.where(later, c0, 0.0), jnp.where(later, c1, 0.0)
            blocks[i] = blocks[i] - (c0 * x0 + c1 * x1)
            duals[i] = duals[i] - (c0 * y0 + c1 * y1)


def basis_kernel(p_ref, u_ref, inverse):
    rank = p_ref.shape[1]
    rows = lax.broadcasted_iota(jnp.int32, (rank, rank), 0)
    columns = lax.broadcasted_iota(jnp.int32, (rank, rank), 1)
    eye = jnp.where(rows == columns, 1.0, 0.0).astype(jnp.float32)
    half = jnp.where(rows > columns, 1.0, 0.5 * eye)

    p = p_ref[...]
    p = p * lax.rsqrt(jnp.sum(p * p, axis=0, keepdims=True))
    inverse_factor(dot(p, p, ((0,), (0,))), inverse)
    q = dot(p, inverse[...], ((1,), (1,)))

    a = dot(q, q, ((0,), (0,)))
    e = a - eye
    near = jnp.sum(e * e) < 1e-4

    @pl.when(near)
    def _():
        x = eye - half * e
        e1 = dot(dot(x, a, ((1,), (0,))), x, ((1,), (1,))) - eye
        inverse[...] = x - dot(half * e1, x, ((1,), (0,)))

    @pl.when(jnp.logical_not(near))
    def _():
        inverse_factor(a, inverse)

    u_ref[...] = dot(q, inverse[...], ((1,), (1,)))


def basis(p):
    vmem = pl.BlockSpec(memory_space=pltpu.VMEM)
    rank = p.shape[1]
    return pl.pallas_call(
        basis_kernel,
        out_shape=jax.ShapeDtypeStruct(p.shape, jnp.float32),
        in_specs=[vmem],
        out_specs=vmem,
        scratch_shapes=[pltpu.VMEM((rank, rank), jnp.float32)],
        compiler_params=pltpu.CompilerParams(vmem_limit_bytes=32 * 2**20),
        name="orthonormal_basis",
    )(p)


def core_kernel(modes, parts, u_ref, f_ref, c_ref, local, send, recv, own_sem):
    me = lax.axis_index("mode")
    greet(modes, 1)
    width = f_ref.shape[1]
    cw = width // parts
    rows = c_ref.shape[0]
    ut = u_ref[...].T
    sent = []
    for k in range(parts):
        local[:, pl.ds(k * cw, cw)] = dot(ut, f_ref[:, pl.ds(k * cw, cw)], ((1,), (0,)))
        here = pl.ds(pl.multiple_of(me * width + k * cw, cw), cw)
        for d in range(modes - 1, 0, -1):
            peer = lax.rem(me + d, modes)
            copy = pltpu.make_async_remote_copy(
                src_ref=local.at[pl.ds(pl.multiple_of(peer * rows, rows), rows), pl.ds(k * cw, cw)],
                dst_ref=c_ref.at[:, here],
                send_sem=send.at[k * (modes - 1) + d - 1],
                recv_sem=recv.at[k * (modes - 1) + d - 1],
                device_id={"mode": peer}, device_id_type=MESH,
            )
            copy.start()
            sent.append(copy)
    own = pltpu.make_async_copy(
        local.at[pl.ds(pl.multiple_of(me * rows, rows), rows)],
        c_ref.at[:, pl.ds(pl.multiple_of(me * width, width), width)],
        own_sem,
    )
    own.start()
    own.wait()
    for copy in sent:
        copy.wait()


def core(modes, u, f):
    whole, width = f.shape
    rank = u.shape[1]
    parts = 2 if width % 256 == 0 else 1
    vmem = pl.BlockSpec(memory_space=pltpu.VMEM)
    dma = pltpu.SemaphoreType.DMA
    return pl.pallas_call(
        functools.partial(core_kernel, modes, parts),
        out_shape=jax.ShapeDtypeStruct((rank // modes, width * modes), jnp.float32),
        in_specs=[vmem, vmem],
        out_specs=vmem,
        scratch_shapes=[
            pltpu.VMEM((rank, width), jnp.float32),
            dma((parts * (modes - 1),)), dma((parts * (modes - 1),)),
            dma,
        ],
        compiler_params=pltpu.CompilerParams(
            collective_id=1, has_side_effects=True, vmem_limit_bytes=32 * 2**20
        ),
        name="core_tensor",
    )(u, f)


def solution(mesh):
    modes, cols = mesh.shape["mode"], mesh.shape["cols"]

    def shards(snapshots, start_basis):
        fibres, projected = gather(modes, cols, snapshots, start_basis)
        subspace_basis = basis(projected)
        return subspace_basis, core(modes, subspace_basis, fibres)

    return jax.shard_map(
        shards,
        mesh=mesh,
        in_specs=(P("mode", "cols"), P()),
        out_specs=(P(), P("mode", "cols")),
        check_vma=False,
    )
```

time: 277 us -> 106 us (0.38)
  waiting for transfers between devices: 143 us -> 0 us
  Pallas kernels: 0 us -> 101 us
  blocking collectives: 55.2 us -> 0 us
  other arithmetic: 45.7 us -> 0 us
  between operations: 14.1 us -> 0.66 us
  matrix products: 10.8 us -> 0 us
  starting transfers between devices: 3.56 us -> 0 us
    psum x1 -> x0, waiting for transfers between devices: 129 us -> none  [shards(): gram_whole = lax.psum(local_gram, ('mode', 'cols'))]
    pallas_call x0 -> x3, Pallas kernels: none -> 101 us  [the longest x1 72 us: gather(): pl.pallas_call(functools.partial(gather_kernel, modes, cols, parts), out_...]
    all_to_all x1 -> x0, blocking collectives: 55.2 us -> none  [shards(): lax.all_to_all(snapshots, 'mode', split_axis=1, concat_axis=0, tiled=True)]
    another operation x10 -> x0, other arithmetic: 45.7 us -> none  [the longest x6 24.8 us: orthonormal(): lower_part = jnp.linalg.cholesky(inner)]
    all_to_all x1 -> x0, waiting for transfers between devices: 14.5 us -> none  [shards(): lax.all_to_all(core_local, 'mode', split_axis=0, concat_axis=1, tiled=True)]
    dot_general x5 -> x0, matrix products: 10 us -> none  [the longest x1 4.56 us: shards(): jnp.dot(fibres, fibres.T, precision=lax.Precision.HIGHEST, preferred_elem...]
    all_to_all x1 -> x0, starting transfers between devices: 3.52 us -> none  [shards(): lax.all_to_all(core_local, 'mode', split_axis=0, concat_axis=1, tiled=True)]
    unnamed x3 -> x7, local copies, waits for them, and re-layouts: 0.84 us -> 4.28 us
  transfers between devices with their start and end apart: 2 -> 0, of which waited for: 2 -> 0; matrix products, arithmetic and copies ran while one was open for 0% -> 0% of each run, Pallas kernels for 0% -> 0%
where the time goes in v1:
time: 106 us
  Pallas kernels  101 us (95%)
  local copies, waits for them, and re-layouts  4.28 us (4%)
    pallas_call x1, Pallas kernels, gather(): pl.pallas_call(functools.partial(gather_kernel, modes, cols, parts), out_...  72 us
    pallas_call x1, Pallas kernels, core(): pl.pallas_call(functools.partial(core_kernel, modes, parts), out_shape=ja...  16.1 us
    pallas_call x1, Pallas kernels, basis(): pl.pallas_call(basis_kernel, out_shape=jax.ShapeDtypeStruct(p.shape, jnp....  13.1 us
    unnamed x7, local copies, waits for them, and re-layouts  4.28 us

profile of v1, /device:TPU:0, one launch (start us, length us, event | category | flops | bytes accessed | tf_op | source)
XLA Modules:
  0.0 106.1 jit_solution(8394807823488697378)
XLA Ops:
  0.6 0.0 copy-start
  0.6 1.6 %copy-done = f32[64,8192]{1,0:T(8,128)S(1)} copy-done((f32[64,8192]{1,0:T(8,128)S(1)}, f32[64,8192]{1,0:T(8,128)}, u32[]{:S(2)}) %copy-start) | copy-done | bytes 2097176
  2.2 0.0 copy-start.2
  2.2 0.9 copy-done.2
  3.2 72.0 %gather_project.1 = (f32[512,1024]{1,0:T(8,128)S(1)}, f32[512,128]{1,0:T(8,128)S(1)}) custom-call(f32[64,8192]{1,0:T(8,128)S(1)} %copy-done, f32[512,128]{1,0:T(8,128)S(1)} %copy-done.2), custom_call_target="tpu_custom_call" | custom-call | tf_op jit(solution)/shard_map/gather_project/pallas_call | solution.py:186
  75.2 13.1 %orthonormal_basis.1.u_ref = f32[512,128]{1,0:T(8,128)} custom-call(f32[512,128]{1,0:T(8,128)S(1)} %get-tuple-element.4.p_ref), custom_call_target="tpu_custom_call" | custom-call | tf_op jit(solution)/shard_map/orthonormal_basis/pallas_call | solution.py:281
  88.3 0.0 copy-start.1
  88.3 0.9 copy-done.1
  89.2 16.1 %core_tensor.1 = f32[16,8192]{1,0:T(8,128)S(1)} custom-call(f32[512,128]{1,0:T(8,128)S(1)} %copy-done.1, f32[512,1024]{1,0:T(8,128)S(1)} %get-tuple-element.5.f_ref), custom_call_target="tpu_custom_call" | custom-call | tf_op jit(solution)/shard_map/core_tensor/pallas_call | solution.py:331
  105.3 0.8 copy.5
Async XLA Ops:
  0.6 1.6 %copy-start = (f32[64,8192]{1,0:T(8,128)S(1)}, f32[64,8192]{1,0:T(8,128)}, u32[]{:S(2)}) copy-start(f32[64,8192]{1,0:T(8,128)} %x_ref.1) | copy-start | bytes 6291460
  2.2 0.9 copy-start.2
  88.3 0.9 copy-start.1

commit v2 on v1

--- a/solution.py
+++ b/solution.py
@@ -21,6 +21,22 @@
     )
 
 
+def pairing(me, d, modes):
+    if modes & (modes - 1):
+        return lax.rem(me + d, modes)
+    peer = me
+    bit = 1
+    while bit < modes:
+        if d & bit:
+            peer = peer + bit * (1 - 2 * lax.rem(me // bit, 2))
+        bit *= 2
+    return peer
+
+
+def small(a, b, dims):
+    return lax.dot_general(a, b, (dims, ((), ())), preferred_element_type=jnp.float32)
+
+
 def greet(modes, cols):
     me, mc = lax.axis_index("mode"), lax.axis_index("cols")
     barrier = pltpu.get_barrier_semaphore()
@@ -32,14 +48,14 @@
         pl.semaphore_signal(
             barrier, inc=1, device_id={"cols": lax.rem(mc + d, cols)}, device_id_type=MESH
         )
-    pl.semaphore_wait(barrier, modes - 1 + cols - 1)
+    return lambda: pl.semaphore_wait(barrier, modes - 1 + cols - 1)
 
 
 def gather_kernel(
     modes, cols, parts,
     x_ref, b_ref, f_ref, p_ref,
-    part, piece, slots_c, slots_m,
-    own_sem, s0, r0, s1, r1, s2, r2, s3, r3, s4, r4,
+    basis, part, piece, slots_c, slots_m,
+    own_sem, basis_sem, s0, r0, s1, r1, s2, r2, s3, r3, s4, r4,
 ):
     me, mc = lax.axis_index("mode"), lax.axis_index("cols")
     rows = x_ref.shape[0]
@@ -54,6 +70,9 @@
         )
 
     my_rows = pl.ds(pl.multiple_of(me * rows, rows), rows)
+    everyone = greet(modes, cols)
+    start = pltpu.make_async_copy(b_ref, basis, basis_sem)
+    start.start()
     own = []
     for k in range(parts):
         copy = pltpu.make_async_copy(
@@ -64,23 +83,31 @@
         copy.start()
         own.append(copy)
 
-    greet(modes, cols)
-
-    sent = []
-    for k in range(parts):
-        row = []
-        for d in range(modes - 1, 0, -1):
-            peer = lax.rem(me + d, modes)
+    everyone()
+
+    sent = [[] for _ in range(parts)]
+
+    def send(k, rounds):
+        for d in rounds:
+            peer = pairing(me, d, modes)
             copy = put(
                 x_ref.at[:, pl.ds(pl.multiple_of(peer * width + k * cw, cw), cw)],
                 f_ref.at[my_rows, pl.ds(k * cw, cw)],
                 s0.at[k * (modes - 1) + d - 1], r0.at[k * (modes - 1) + d - 1], "mode", peer,
             )
             copy.start()
-            row.append(copy)
-        sent.append(row)
-
-    bt = b_ref[...].T
+            sent[k].append(copy)
+
+    far = range(modes - 1, modes // 2 - 1, -1)
+    near = range(modes // 2 - 1, 0, -1)
+    for k in range(parts):
+        send(k, far)
+        if k > 0:
+            send(k - 1, near)
+    send(parts - 1, near)
+
+    start.wait()
+    bt = basis[...].T
     for k in range(parts):
         own[k].wait()
         for copy in sent[k]:
@@ -121,8 +148,8 @@
             pl.when(flag)(body)
 
     second = []
-    for d in range(1, modes):
-        peer = lax.rem(me + d, modes)
+    for d in range(modes - 1, 0, -1):
+        peer = pairing(me, d, modes)
         place = peer if owners == modes else lax.rem(peer, owners)
         copy = put(
             piece.at[pl.ds(pl.multiple_of(place * sl, sl), sl)],
@@ -144,22 +171,32 @@
     guarded(me < owners, add)
 
     third = []
-    for d in range(1, modes):
-        peer = lax.rem(me + d, modes)
+    for d in range(modes - 1, 0, -1):
+        peer = pairing(me, d, modes)
         copy = put(p_ref.at[target], p_ref.at[target], s3.at[d - 1], r3.at[d - 1], "mode", peer)
         guarded(me < owners, copy.start)
         third.append(copy)
+    fourth = []
+
+    def forward(d, source):
+        spot = source if owners == modes else lax.rem(source, owners)
+        rows_of = pl.ds(pl.multiple_of(mc * rc + spot * sl, sl), sl)
+        for e in range(1, cols):
+            at = d * (cols - 1) + e - 1
+            copy = put(
+                p_ref.at[rows_of], p_ref.at[rows_of], s4.at[at], r4.at[at],
+                "cols", lax.rem(mc + e, cols),
+            )
+            guarded(source < owners, copy.start)
+            fourth.append((copy, source))
+
+    forward(0, me)
     for d in range(1, modes):
-        source = lax.rem(me + modes - d, modes)
-        guarded(source < owners, third[d - 1].wait_recv)
-    fourth = []
-    for d in range(1, cols):
-        peer = lax.rem(mc + d, cols)
-        copy = put(p_ref.at[mine], p_ref.at[mine], s4.at[d - 1], r4.at[d - 1], "cols", peer)
-        copy.start()
-        fourth.append(copy)
-    for copy in fourth:
-        copy.wait_recv()
+        source = pairing(me, d, modes) if modes & (modes - 1) == 0 else lax.rem(me + modes - d, modes)
+        guarded(source < owners, third[modes - 1 - d].wait_recv)
+        forward(d, source)
+    for copy, source in fourth:
+        guarded(source < owners, copy.wait_recv)
 
     for row in sent:
         for copy in row:
@@ -170,15 +207,15 @@
         guarded(peer < owners, copy.wait_send)
     for copy in third:
         guarded(me < owners, copy.wait_send)
-    for copy in fourth:
-        copy.wait_send()
+    for copy, source in fourth:
+        guarded(source < owners, copy.wait_send)
 
 
 def gather(modes, cols, x, b):
     rows, local = x.shape
     whole, width = rows * modes, local // modes
     rank = b.shape[1]
-    parts = 2 if width % 256 == 0 else 1
+    parts = 4 if width % 512 == 0 else 1
     rc = whole // cols
     sl = max(SUB, rc // modes)
     dma = pltpu.SemaphoreType.DMA
@@ -189,19 +226,20 @@
             jax.ShapeDtypeStruct((whole, width), jnp.float32),
             jax.ShapeDtypeStruct((whole, rank), jnp.float32),
         ),
-        in_specs=[pl.BlockSpec(memory_space=pl.ANY), vmem],
+        in_specs=[pl.BlockSpec(memory_space=pltpu.HBM)] * 2,
         out_specs=(vmem, vmem),
         scratch_shapes=[
+            pltpu.VMEM((whole, rank), jnp.float32),
             pltpu.VMEM((whole, rank), jnp.float32),
             pltpu.VMEM((rc, rank), jnp.float32),
             pltpu.VMEM((cols - 1, rc, rank), jnp.float32),
             pltpu.VMEM((modes - 1, sl, rank), jnp.float32),
-            dma((parts,)),
+            dma((parts,)), dma,
             dma((parts * (modes - 1),)), dma((parts * (modes - 1),)),
             dma((cols - 1,)), dma((cols - 1,)),
             dma((modes - 1,)), dma((modes - 1,)),
             dma((modes - 1,)), dma((modes - 1,)),
-            dma((cols - 1,)), dma((cols - 1,)),
+            dma((modes * (cols - 1),)), dma((modes * (cols - 1),)),
         ],
         compiler_params=pltpu.CompilerParams(
             collective_id=0, has_side_effects=True, vmem_limit_bytes=32 * 2**20
@@ -246,7 +284,7 @@
             duals[i] = duals[i] - (c0 * y0 + c1 * y1)
 
 
-def basis_kernel(p_ref, u_ref, inverse):
+def basis_kernel(p_ref, u_ref, ut_ref, inverse):
     rank = p_ref.shape[1]
     rows = lax.broadcasted_iota(jnp.int32, (rank, rank), 0)
     columns = lax.broadcasted_iota(jnp.int32, (rank, rank), 1)
@@ -260,19 +298,23 @@
 
     a = dot(q, q, ((0,), (0,)))
     e = a - eye
-    near = jnp.sum(e * e) < 1e-4
+    near = jnp.sum(e * e) < 1e-6
 
     @pl.when(near)
     def _():
-        x = eye - half * e
-        e1 = dot(dot(x, a, ((1,), (0,))), x, ((1,), (1,))) - eye
-        inverse[...] = x - dot(half * e1, x, ((1,), (0,)))
+        low = half * e
+        m = small(low, e, ((1,), (0,)))
+        e1 = small(low + m, low, ((1,), (1,))) - m - m.T
+        low1 = half * e1
+        step = low + low1 - small(low1, low, ((1,), (0,)))
+        u_ref[...] = q - small(q, step, ((1,), (1,)))
 
     @pl.when(jnp.logical_not(near))
     def _():
         inverse_factor(a, inverse)
-
-    u_ref[...] = dot(q, inverse[...], ((1,), (1,)))
+        u_ref[...] = dot(q, inverse[...], ((1,), (1,)))
+
+    ut_ref[...] = u_ref[...].T
 
 
 def basis(p):
@@ -280,28 +322,32 @@
     rank = p.shape[1]
     return pl.pallas_call(
         basis_kernel,
-        out_shape=jax.ShapeDtypeStruct(p.shape, jnp.float32),
+        out_shape=(
+            jax.ShapeDtypeStruct(p.shape, jnp.float32),
+            jax.ShapeDtypeStruct((rank, p.shape[0]), jnp.float32),
+        ),
         in_specs=[vmem],
-        out_specs=vmem,
+        out_specs=(vmem, vmem),
         scratch_shapes=[pltpu.VMEM((rank, rank), jnp.float32)],
         compiler_params=pltpu.CompilerParams(vmem_limit_bytes=32 * 2**20),
         name="orthonormal_basis",
     )(p)
 
 
-def core_kernel(modes, parts, u_ref, f_ref, c_ref, local, send, recv, own_sem):
+def core_kernel(modes, parts, ut_ref, f_ref, c_ref, local, send, recv, own_sem):
     me = lax.axis_index("mode")
-    greet(modes, 1)
+    everyone = greet(modes, 1)
     width = f_ref.shape[1]
     cw = width // parts
     rows = c_ref.shape[0]
-    ut = u_ref[...].T
     sent = []
     for k in range(parts):
-        local[:, pl.ds(k * cw, cw)] = dot(ut, f_ref[:, pl.ds(k * cw, cw)], ((1,), (0,)))
+        local[:, pl.ds(k * cw, cw)] = dot(ut_ref[...], f_ref[:, pl.ds(k * cw, cw)], ((1,), (0,)))
+        if k == 0:
+            everyone()
         here = pl.ds(pl.multiple_of(me * width + k * cw, cw), cw)
         for d in range(modes - 1, 0, -1):
-            peer = lax.rem(me + d, modes)
+            peer = pairing(me, d, modes)
             copy = pltpu.make_async_remote_copy(
                 src_ref=local.at[pl.ds(pl.multiple_of(peer * rows, rows), rows), pl.ds(k * cw, cw)],
                 dst_ref=c_ref.at[:, here],
@@ -322,10 +368,10 @@
         copy.wait()
 
 
-def core(modes, u, f):
+def core(modes, ut, f):
     whole, width = f.shape
-    rank = u.shape[1]
-    parts = 2 if width % 256 == 0 else 1
+    rank = ut.shape[0]
+    parts = 4 if width % 512 == 0 else 1
     vmem = pl.BlockSpec(memory_space=pltpu.VMEM)
     dma = pltpu.SemaphoreType.DMA
     return pl.pallas_call(
@@ -342,7 +388,7 @@
             collective_id=1, has_side_effects=True, vmem_limit_bytes=32 * 2**20
         ),
         name="core_tensor",
-    )(u, f)
+    )(ut, f)
 
 
 def solution(mesh):
@@ -350,8 +396,8 @@
 
     def shards(snapshots, start_basis):
         fibres, projected = gather(modes, cols, snapshots, start_basis)
-        subspace_basis = basis(projected)
-        return subspace_basis, core(modes, subspace_basis, fibres)
+        subspace_basis, transposed = basis(projected)
+        return subspace_basis, core(modes, transposed, fibres)
 
     return jax.shard_map(
         shards,

time: 106 us -> 103 us (0.972)
  Pallas kernels: 101 us -> 98.5 us
    pallas_call x1, Pallas kernels: 72 us -> 70.3 us  [gather(): pl.pallas_call(functools.partial(gather_kernel, modes, cols, parts), out_...]
    unnamed x7 -> x5, local copies, waits for them, and re-layouts: 4.28 us -> 3.33 us
where the time goes in v2:
time: 103 us
  Pallas kernels  98.5 us (96%)
  local copies, waits for them, and re-layouts  3.33 us (3%)
    pallas_call x1, Pallas kernels, gather(): pl.pallas_call(functools.partial(gather_kernel, modes, cols, parts), out_...  70.3 us
    pallas_call x1, Pallas kernels, core(): pl.pallas_call(functools.partial(core_kernel, modes, parts), out_shape=ja...  15.8 us
    pallas_call x1, Pallas kernels, basis(): pl.pallas_call(basis_kernel, out_shape=(jax.ShapeDtypeStruct(p.shape, jnp...  12.5 us
    unnamed x5, local copies, waits for them, and re-layouts  3.33 us

profile of v2, /device:TPU:0, one launch (start us, length us, event | category | flops | bytes accessed | tf_op | source)
XLA Modules:
  0.0 102.5 jit_solution(12301934805563143474)
XLA Ops:
  0.6 0.0 copy-start
  0.6 1.6 %copy-done = f32[64,8192]{1,0:T(8,128)S(1)} copy-done((f32[64,8192]{1,0:T(8,128)S(1)}, f32[64,8192]{1,0:T(8,128)}, u32[]{:S(2)}) %copy-start) | copy-done | bytes 2097176
  2.2 0.0 copy-start.1
  2.2 0.9 copy-done.1
  3.2 70.3 %gather_project.1 = (f32[512,1024]{1,0:T(8,128)S(1)}, f32[512,128]{1,0:T(8,128)S(1)}) custom-call(f32[64,8192]{1,0:T(8,128)S(1)} %copy-done, f32[512,128]{1,0:T(8,128)S(1)} %copy-done.1), custom_call_target="tpu_custom_call" | custom-call | tf_op jit(solution)/shard_map/gather_project/pallas_call | solution.py:223
  73.4 12.5 %orthonormal_basis.1 = (f32[512,128]{1,0:T(8,128)}, f32[128,512]{1,0:T(8,128)S(1)}) custom-call(f32[512,128]{1,0:T(8,128)S(1)} %get-tuple-element.6.p_ref), custom_call_target="tpu_custom_call" | custom-call | tf_op jit(solution)/shard_map/orthonormal_basis/pallas_call | solution.py:323
  86.0 15.8 %core_tensor.1 = f32[16,8192]{1,0:T(8,128)S(1)} custom-call(f32[128,512]{1,0:T(8,128)S(1)} %get-tuple-element.8.ut_ref, f32[512,1024]{1,0:T(8,128)S(1)} %get-tuple-element.9.f_ref), custom_call_target="tpu_custom_call" | custom-call | tf_op jit(solution)/shard_map/core_tensor/pallas_call | solution.py:377
  101.7 0.8 copy.5
Async XLA Ops:
  0.6 1.6 %copy-start = (f32[64,8192]{1,0:T(8,128)S(1)}, f32[64,8192]{1,0:T(8,128)}, u32[]{:S(2)}) copy-start(f32[64,8192]{1,0:T(8,128)} %x_ref.1) | copy-start | bytes 6291460
  2.2 0.9 copy-start.1

commit v3 on v2

--- a/solution.py
+++ b/solution.py
@@ -248,6 +248,12 @@
     )(x, b)
 
 
+def tree(terms):
+    while len(terms) > 1:
+        terms = [sum(terms[i:i + 2][1:], terms[i]) for i in range(0, len(terms), 2)]
+    return terms[0]
+
+
 def inverse_factor(a, out_ref):
     n = a.shape[0]
     count = n // SUB
@@ -258,30 +264,49 @@
     duals = [
         jnp.where(col_id == row_id + SUB * i, 1.0, 0.0).astype(jnp.float32) for i in range(count)
     ]
-    for j in range(0, n, 2):
-        at, jj = j // SUB, j % SUB
-        block, dual = blocks[at], duals[at]
-        u0, u1 = (jnp.broadcast_to(block[jj + i:jj + i + 1, :], shape) for i in range(2))
-        v0, v1 = (jnp.broadcast_to(dual[jj + i:jj + i + 1, :], shape) for i in range(2))
-        p = jnp.broadcast_to(u0[:, j:j + 1], shape)
-        q = jnp.broadcast_to(u0[:, j + 1:j + 2], shape)
-        r = jnp.broadcast_to(u1[:, j + 1:j + 2], shape)
-        idet = 1.0 / (p * r - q * q)
-        i00, i01, i11 = r * idet, -q * idet, p * idet
-        x0, x1 = i00 * u0 + i01 * u1, i01 * u0 + i11 * u1
-        y0, y1 = i00 * v0 + i01 * v1, i01 * v0 + i11 * v1
-        out_ref[j:j + 1, :] = (v0 * lax.rsqrt(p))[0:1, :]
-        out_ref[j + 1:j + 2, :] = ((v1 - (q / p) * v0) * jnp.sqrt(i11))[0:1, :]
-        for i in range(at, count):
-            c0 = jnp.broadcast_to(blocks[i][:, j:j + 1], shape)
-            c1 = jnp.broadcast_to(blocks[i][:, j + 1:j + 2], shape)
-            if i == at:
-                if jj + 2 == SUB:
-                    continue
-                later = row_id > jj + 1
-                c0, c1 = jnp.where(later, c0, 0.0), jnp.where(later, c1, 0.0)
-            blocks[i] = blocks[i] - (c0 * x0 + c1 * x1)
-            duals[i] = duals[i] - (c0 * y0 + c1 * y1)
+
+    def row(block, i):
+        return jnp.broadcast_to(block[i:i + 1, :], shape)
+
+    def column(block, j):
+        return jnp.broadcast_to(block[:, j:j + 1], shape)
+
+    for at in range(count):
+        base = SUB * at
+        diagonal = [column(blocks[at], base + k) for k in range(SUB)]
+        block, dual, lower = blocks[at], duals[at], duals[at]
+        for k in range(0, SUB, 2):
+            c0, c1 = diagonal[k], diagonal[k + 1]
+            p, q, r = row(c0, k), row(c1, k), row(c1, k + 1)
+            idet = 1.0 / (p * r - q * q)
+            i00, i01, i11 = r * idet, -q * idet, p * idet
+
+            def solve(m):
+                m0, m1 = row(m, k), row(m, k + 1)
+                return i00 * m0 + i01 * m1, i01 * m0 + i11 * m1
+
+            def step(m):
+                x0, x1 = solve(m)
+                rest = m - (c0 * x0 + c1 * x1)
+                return jnp.where(row_id == k, x0, jnp.where(row_id == k + 1, x1, rest))
+
+            for later in range(k + 2, SUB):
+                diagonal[later] = step(diagonal[later])
+            v0, v1 = row(lower, k), row(lower, k + 1)
+            out_ref[base + k:base + k + 1, :] = (v0 * lax.rsqrt(p))[0:1, :]
+            out_ref[base + k + 1:base + k + 2, :] = ((v1 - (q / p) * v0) * jnp.sqrt(i11))[0:1, :]
+            if k + 2 < SUB:
+                y0, y1 = solve(lower)
+                lower = jnp.where(row_id > k + 1, lower - (c0 * y0 + c1 * y1), lower)
+            block, dual = step(block), step(dual)
+        if at + 1 == count:
+            break
+        xs = [row(block, k) for k in range(SUB)]
+        ys = [row(dual, k) for k in range(SUB)]
+        for i in range(at + 1, count):
+            cs = [column(blocks[i], base + k) for k in range(SUB)]
+            blocks[i] = blocks[i] - tree([c * x for c, x in zip(cs, xs)])
+            duals[i] = duals[i] - tree([c * y for c, y in zip(cs, ys)])
 
 
 def basis_kernel(p_ref, u_ref, ut_ref, inverse):

time: 103 us -> 98.2 us (0.953)
  Pallas kernels: 98.5 us -> 94 us
    pallas_call x1, Pallas kernels: 12.5 us -> 7.98 us  [basis(): pl.pallas_call(basis_kernel, out_shape=(jax.ShapeDtypeStruct(p.shape, jnp...]
where the time goes in v3:
time: 98.2 us; the launch traced here: 98 us
  Pallas kernels  94 us (96%)
  local copies, waits for them, and re-layouts  3.33 us (3%)
    pallas_call x1, Pallas kernels, gather(): pl.pallas_call(functools.partial(gather_kernel, modes, cols, parts), out_...  70.3 us
    pallas_call x1, Pallas kernels, core(): pl.pallas_call(functools.partial(core_kernel, modes, parts), out_shape=ja...  15.8 us
    pallas_call x1, Pallas kernels, basis(): pl.pallas_call(basis_kernel, out_shape=(jax.ShapeDtypeStruct(p.shape, jnp...  7.98 us
    unnamed x5, local copies, waits for them, and re-layouts  3.33 us

profile of v3, /device:TPU:0, one launch (start us, length us, event | category | flops | bytes accessed | tf_op | source)
XLA Modules:
  0.0 98.0 jit_solution(4801156015402375556)
XLA Ops:
  0.6 0.0 copy-start
  0.6 1.6 %copy-done = f32[64,8192]{1,0:T(8,128)S(1)} copy-done((f32[64,8192]{1,0:T(8,128)S(1)}, f32[64,8192]{1,0:T(8,128)}, u32[]{:S(2)}) %copy-start) | copy-done | bytes 2097176
  2.2 0.0 copy-start.1
  2.2 0.9 copy-done.1
  3.2 70.3 %gather_project.1 = (f32[512,1024]{1,0:T(8,128)S(1)}, f32[512,128]{1,0:T(8,128)S(1)}) custom-call(f32[64,8192]{1,0:T(8,128)S(1)} %copy-done, f32[512,128]{1,0:T(8,128)S(1)} %copy-done.1), custom_call_target="tpu_custom_call" | custom-call | tf_op jit(solution)/shard_map/gather_project/pallas_call | solution.py:223
  73.4 8.0 %orthonormal_basis.1 = (f32[512,128]{1,0:T(8,128)}, f32[128,512]{1,0:T(8,128)S(1)}) custom-call(f32[512,128]{1,0:T(8,128)S(1)} %get-tuple-element.6.p_ref), custom_call_target="tpu_custom_call" | custom-call | tf_op jit(solution)/shard_map/orthonormal_basis/pallas_call | solution.py:348
  81.4 15.8 %core_tensor.1 = f32[16,8192]{1,0:T(8,128)S(1)} custom-call(f32[128,512]{1,0:T(8,128)S(1)} %get-tuple-element.8.ut_ref, f32[512,1024]{1,0:T(8,128)S(1)} %get-tuple-element.9.f_ref), custom_call_target="tpu_custom_call" | custom-call | tf_op jit(solution)/shard_map/core_tensor/pallas_call | solution.py:402
  97.2 0.8 copy.5
Async XLA Ops:
  0.6 1.6 %copy-start = (f32[64,8192]{1,0:T(8,128)S(1)}, f32[64,8192]{1,0:T(8,128)}, u32[]{:S(2)}) copy-start(f32[64,8192]{1,0:T(8,128)} %x_ref.1) | copy-start | bytes 6291460
  2.2 0.9 copy-start.1

commit v4 on v3

--- a/solution.py
+++ b/solution.py
@@ -366,12 +366,12 @@
     cw = width // parts
     rows = c_ref.shape[0]
     sent = []
-    for k in range(parts):
-        local[:, pl.ds(k * cw, cw)] = dot(ut_ref[...], f_ref[:, pl.ds(k * cw, cw)], ((1,), (0,)))
-        if k == 0:
-            everyone()
+    far = range(modes - 1, modes // 2 - 1, -1)
+    near = range(modes // 2 - 1, 0, -1)
+
+    def deliver(k, rounds):
         here = pl.ds(pl.multiple_of(me * width + k * cw, cw), cw)
-        for d in range(modes - 1, 0, -1):
+        for d in rounds:
             peer = pairing(me, d, modes)
             copy = pltpu.make_async_remote_copy(
                 src_ref=local.at[pl.ds(pl.multiple_of(peer * rows, rows), rows), pl.ds(k * cw, cw)],
@@ -382,6 +382,15 @@
             )
             copy.start()
             sent.append(copy)
+
+    for k in range(parts):
+        local[:, pl.ds(k * cw, cw)] = dot(ut_ref[...], f_ref[:, pl.ds(k * cw, cw)], ((1,), (0,)))
+        if k == 0:
+            everyone()
+        deliver(k, far)
+        if k > 0:
+            deliver(k - 1, near)
+    deliver(parts - 1, near)
     own = pltpu.make_async_copy(
         local.at[pl.ds(pl.multiple_of(me * rows, rows), rows)],
         c_ref.at[:, pl.ds(pl.multiple_of(me * width, width), width)],

time: 98.2 us -> 98.2 us (level)
  no operation moved by 1% of the time
where the time goes in v4:
time: 98.2 us; the launch traced here: 98 us
  Pallas kernels  94 us (96%)
  local copies, waits for them, and re-layouts  3.33 us (3%)
    pallas_call x1, Pallas kernels, gather(): pl.pallas_call(functools.partial(gather_kernel, modes, cols, parts), out_...  70.3 us
    pallas_call x1, Pallas kernels, core(): pl.pallas_call(functools.partial(core_kernel, modes, parts), out_shape=ja...  15.8 us
    pallas_call x1, Pallas kernels, basis(): pl.pallas_call(basis_kernel, out_shape=(jax.ShapeDtypeStruct(p.shape, jnp...  7.98 us
    unnamed x5, local copies, waits for them, and re-layouts  3.33 us

profile of v4, /device:TPU:0, one launch (start us, length us, event | category | flops | bytes accessed | tf_op | source)
XLA Modules:
  0.0 98.0 jit_solution(1070348860124294577)
XLA Ops:
  0.6 0.0 copy-start
  0.6 1.6 %copy-done = f32[64,8192]{1,0:T(8,128)S(1)} copy-done((f32[64,8192]{1,0:T(8,128)S(1)}, f32[64,8192]{1,0:T(8,128)}, u32[]{:S(2)}) %copy-start) | copy-done | bytes 2097176
  2.2 0.0 copy-start.1
  2.2 0.9 copy-done.1
  3.2 70.3 %gather_project.1 = (f32[512,1024]{1,0:T(8,128)S(1)}, f32[512,128]{1,0:T(8,128)S(1)}) custom-call(f32[64,8192]{1,0:T(8,128)S(1)} %copy-done, f32[512,128]{1,0:T(8,128)S(1)} %copy-done.1), custom_call_target="tpu_custom_call" | custom-call | tf_op jit(solution)/shard_map/gather_project/pallas_call | solution.py:223
  73.4 8.0 %orthonormal_basis.1 = (f32[512,128]{1,0:T(8,128)}, f32[128,512]{1,0:T(8,128)S(1)}) custom-call(f32[512,128]{1,0:T(8,128)S(1)} %get-tuple-element.6.p_ref), custom_call_target="tpu_custom_call" | custom-call | tf_op jit(solution)/shard_map/orthonormal_basis/pallas_call | solution.py:348
  81.4 15.8 %core_tensor.1 = f32[16,8192]{1,0:T(8,128)S(1)} custom-call(f32[128,512]{1,0:T(8,128)S(1)} %get-tuple-element.8.ut_ref, f32[512,1024]{1,0:T(8,128)S(1)} %get-tuple-element.9.f_ref), custom_call_target="tpu_custom_call" | custom-call | tf_op jit(solution)/shard_map/core_tensor/pallas_call | solution.py:411
  97.2 0.8 copy.5
Async XLA Ops:
  0.6 1.6 %copy-start = (f32[64,8192]{1,0:T(8,128)S(1)}, f32[64,8192]{1,0:T(8,128)}, u32[]{:S(2)}) copy-start(f32[64,8192]{1,0:T(8,128)} %x_ref.1) | copy-start | bytes 6291460
  2.2 0.9 copy-start.1

commit v5 on v3

--- a/solution.py
+++ b/solution.py
@@ -114,6 +114,8 @@
             copy.wait_recv()
         fk = f_ref[:, pl.ds(k * cw, cw)]
         t = dot(bt, fk, ((1,), (0,)))
+        if k == parts - 1:
+            break
         term = dot(fk, t, ((1,), (1,)))
         if k == 0:
             part[...] = term
@@ -122,15 +124,21 @@
 
     rc = whole // cols
     mine = pl.ds(pl.multiple_of(mc * rc, rc), rc)
+    def last(rows_of):
+        term = dot(f_ref[rows_of, pl.ds(width - cw, cw)], t, ((1,), (1,)))
+        part[rows_of, :] = term if parts == 1 else part[rows_of, :] + term
+
     first = []
     for d in range(1, cols):
         peer = lax.rem(mc + d, cols)
+        last(pl.ds(pl.multiple_of(peer * rc, rc), rc))
         copy = put(
             part.at[pl.ds(pl.multiple_of(peer * rc, rc), rc)],
             slots_c.at[d - 1], s1.at[d - 1], r1.at[d - 1], "cols", peer,
         )
         copy.start()
         first.append(copy)
+    last(mine)
     for copy in first:
         copy.wait_recv()
     total = part[mine, :]

time: 98.2 us -> 97.9 us (level)
  no operation moved by 1% of the time
where the time goes in v5:
time: 97.9 us; the launch traced here: 97.7 us
  Pallas kernels  93.7 us (96%)
  local copies, waits for them, and re-layouts  3.33 us (3%)
    pallas_call x1, Pallas kernels, gather(): pl.pallas_call(functools.partial(gather_kernel, modes, cols, parts), out_...  70 us
    pallas_call x1, Pallas kernels, core(): pl.pallas_call(functools.partial(core_kernel, modes, parts), out_shape=ja...  15.7 us
    pallas_call x1, Pallas kernels, basis(): pl.pallas_call(basis_kernel, out_shape=(jax.ShapeDtypeStruct(p.shape, jnp...  7.99 us
    unnamed x5, local copies, waits for them, and re-layouts  3.33 us

profile of v5, /device:TPU:0, one launch (start us, length us, event | category | flops | bytes accessed | tf_op | source)
XLA Modules:
  0.0 97.7 jit_solution(11361104547544991185)
XLA Ops:
  0.6 0.0 copy-start
  0.6 1.6 %copy-done = f32[64,8192]{1,0:T(8,128)S(1)} copy-done((f32[64,8192]{1,0:T(8,128)S(1)}, f32[64,8192]{1,0:T(8,128)}, u32[]{:S(2)}) %copy-start) | copy-done | bytes 2097176
  2.2 0.0 copy-start.1
  2.2 0.9 copy-done.1
  3.2 70.0 %gather_project.1 = (f32[512,1024]{1,0:T(8,128)S(1)}, f32[512,128]{1,0:T(8,128)S(1)}) custom-call(f32[64,8192]{1,0:T(8,128)S(1)} %copy-done, f32[512,128]{1,0:T(8,128)S(1)} %copy-done.1), custom_call_target="tpu_custom_call" | custom-call | tf_op jit(solution)/shard_map/gather_project/pallas_call | solution.py:231
  73.2 8.0 %orthonormal_basis.1 = (f32[512,128]{1,0:T(8,128)}, f32[128,512]{1,0:T(8,128)S(1)}) custom-call(f32[512,128]{1,0:T(8,128)S(1)} %get-tuple-element.6.p_ref), custom_call_target="tpu_custom_call" | custom-call | tf_op jit(solution)/shard_map/orthonormal_basis/pallas_call | solution.py:356
  81.2 15.7 %core_tensor.1 = f32[16,8192]{1,0:T(8,128)S(1)} custom-call(f32[128,512]{1,0:T(8,128)S(1)} %get-tuple-element.8.ut_ref, f32[512,1024]{1,0:T(8,128)S(1)} %get-tuple-element.9.f_ref), custom_call_target="tpu_custom_call" | custom-call | tf_op jit(solution)/shard_map/core_tensor/pallas_call | solution.py:410
  96.9 0.8 copy.5
Async XLA Ops:
  0.6 1.6 %copy-start = (f32[64,8192]{1,0:T(8,128)S(1)}, f32[64,8192]{1,0:T(8,128)}, u32[]{:S(2)}) copy-start(f32[64,8192]{1,0:T(8,128)} %x_ref.1) | copy-start | bytes 6291460
  2.2 0.9 copy-start.1
